TPU v7x, 32 devices: a whole 2x2x4 slice. The times are simulated.
32 devices in a mesh: parts: 2 (over x), expert: 16 (over z, y, core).
Axes of the slice: x: 2, y: 2, z: 4, core: 2. Of those that a mesh axis runs over, the one named last changes fastest.
Arguments:
- tokens: bfloat16 [256, 4096], P(('parts', 'expert')), parts along dimension 0, may hold values from -6 to 6
- assignments: int32 [256, 8], P(('parts', 'expert')), parts along dimension 0, may hold values from 0 to 3, as said below
- router_gates: float32 [256, 8], P(('parts', 'expert')), parts along dimension 0, may hold values from 0.05 to 0.5
- replica_plan: int32 [4], replicated, may hold values from 0 to 1, as said below
- expert_bias: float32 [2, 4096], replicated, may hold values from -3 to 3
- gate_weight: bfloat16 [16, 4096, 384], P('expert'), may hold values from -0.09375 to 0.09375
- up_weight: bfloat16 [16, 4096, 384], P('expert'), may hold values from -0.09375 to 0.09375
- down_weight: bfloat16 [16, 4096, 384], P('expert'), may hold values from -0.15625 to 0.15625
Outputs:
- expert_mix: bfloat16 [256, 4096], P(('parts', 'expert')), parts along dimension 0
There are 2 independent parts, one for each index of `parts`. A program takes and returns all parts, laid end to end along the dimension named above; an argument that names none is the same for every part. Nothing has to cross between parts.
Inputs may be any that keep to these rules, and one draw needn't show every extreme that they name: `assignments`: in each aligned block of 8 tokens, no replica is named by more than 40 of the block's entries, and some replica is named exactly 40 times in every block. `replica_plan`: every expert is served by at least one replica.
All inputs are finite; a program needn't handle non-finite values.
Results may differ from a plain program's by a relative error of at most 0.0054.
Values may be sent and summed in bfloat16 or wider, within the bound.
A program may use at most 128 MiB of HBM per device.

v0:
```python
import jax
import jax.numpy as jnp
from jax import lax
from jax.sharding import PartitionSpec as P

SPLIT = 4


def local(
    tokens,
    assignments,
    router_gates,
    replica_plan,
    expert_bias,
    gate_weight,
    up_weight,
    down_weight,
):
    devices = lax.axis_size("expert")
    tok_count, top_count = assignments.shape
    model_width = tokens.shape[1]
    expert_count = expert_bias.shape[0]
    replicas = devices // SPLIT
    capacity = 5 * tok_count * top_count * SPLIT // (2 * devices)
    host_gate = gate_weight[0]
    host_up = up_weight[0]
    host_down = down_weight[0]
    pair_index = assignments.reshape(-1)
    onehot = (pair_index[:, None] == jnp.arange(replicas, dtype=jnp.int32)[None, :]).astype(
        jnp.int32
    )
    before = jnp.cumsum(onehot, axis=0) - onehot
    slot_rank = jnp.sum(before * onehot, axis=1)
    copies = jnp.repeat(tokens, top_count, axis=0)
    pair_expert = jnp.sum(onehot * replica_plan[None, :], axis=1)
    expert_pick = (
        pair_expert[:, None] == jnp.arange(expert_count, dtype=jnp.int32)[None, :]
    ).astype(jnp.float32)
    bias_rows = jnp.dot(expert_pick, expert_bias, precision=lax.Precision.HIGHEST)
    buffer = (
        jnp.zeros((replicas, capacity, model_width), jnp.bfloat16)
        .at[pair_index, slot_rank]
        .set(copies)
    )
    outgoing_rows = jnp.broadcast_to(
        buffer[:, None], (replicas, SPLIT, capacity, model_width)
    ).reshape(devices, capacity, model_width)
    received = lax.all_to_all(outgoing_rows, "expert", split_axis=0, concat_axis=0, tiled=True)
    slot_count = received.shape[1]
    rows = received.reshape(-1, model_width)
    gate_pre = jnp.dot(rows, host_gate, preferred_element_type=jnp.float32)
    up_pre = jnp.dot(rows, host_up, preferred_element_type=jnp.float32)
    hidden = (jax.nn.silu(gate_pre) * up_pre).astype(jnp.bfloat16)
    partial_value = lax.dot_general(
        hidden, host_down, (((1,), (1,)), ((), ())), preferred_element_type=jnp.float32
    )
    partial_value = partial_value.astype(jnp.bfloat16).reshape(devices, slot_count, model_width)
    returned = lax.all_to_all(partial_value, "expert", split_axis=0, concat_axis=0, tiled=True)
    gathered = returned.reshape(replicas, SPLIT, capacity, model_width)[pair_index, :, slot_rank, :]
    combined = jnp.sum(gathered.astype(jnp.float32), axis=1)
    with_bias = combined + bias_rows
    weighted = with_bias.reshape(tok_count, top_count, model_width) * router_gates[:, :, None]
    return jnp.sum(weighted, axis=1).astype(jnp.bfloat16)


def solution(mesh):
    in_specs = (
        P(("parts", "expert"), None),
        P(("parts", "expert"), None),
        P(("parts", "expert"), None),
        P(),
        P(),
        P("expert", None, None),
        P("expert", None, None),
        P("expert", None, None),
    )
    out_specs = P(("parts", "expert"), None)
    return jax.shard_map(local, mesh=mesh, in_specs=in_specs, out_specs=out_specs, check_vma=False)
```

profile of v0, /device:TPU:0, one launch (start us, length us, event | category | flops | bytes accessed | tf_op | source)
XLA Modules:
  0.0 303.9 jit_solution(5427275869548171487)
XLA Ops:
  0.0 0.0 copy-start
  0.0 0.9 eq.28
  0.9 0.8 reshape.67
  1.7 0.1 fusion.17
  1.8 1.7 broadcast_bitcast_fusion
  3.5 0.1 reduce_window_sum.11
  3.6 0.8 select_reduce_fusion
  4.5 1.2 broadcast_in_dim.6
  5.7 17.8 %scatter_fusion = bf16[4,40,4096]{2,1,0:T(8,128)(2,1)} fusion(bf16[4,40,4096]{2,1,0:T(8,128)(2,1)} %broadcast_in_dim.6, s32[64]{0:T(128)S(1)} %get-tuple-element.7, bf16[64,4096]{1,0:T(8,128)(2,1)} %broadcast_bitcast_fusion), kind=kCustom, calls=%fused_computation.1 | custom fusion | bytes 1573376 | tf_op jit(solution)/shard_map/scatter | solution.py:43
  23.5 2.0 broadcast_in_dim.8
  25.4 0.0 copy-start.4
  25.4 122.2 %all_to_all.10 = bf16[16,40,4096]{2,1,0:T(8,128)(2,1)S(1)} all-to-all(bf16[16,40,4096]{2,1,0:T(8,128)(2,1)S(1)} %bitcast.41), channel_id=1, replica_groups=mesh['parts'=2,'expert'=16] {'expert'}, dimensions={0} | all-to-all | bytes 10485760 | tf_op jit(solution)/shard_map/all_to_all | solution.py:48
  147.6 0.0 copy-start.1
  147.6 2.3 copy-done.1
  149.9 0.0 copy-done.4
  149.9 3.8 %fusion.5 = f32[640,384]{1,0:T(8,128)} fusion(bf16[640,4096]{1,0:T(8,128)(2,1)S(1)} %bitcast.43, bf16[1,4096,384]{2,1,0:T(8,128)(2,1)S(1)} %copy-done.4), kind=kOutput, calls=%fused_computation.10 | convolution fusion | flops 2013265920 | bytes 9371648 | tf_op jit(solution)/shard_map/dot_general | solution.py:51
  153.7 0.0 copy-done
  153.7 11.6 %convolution_convert_fusion = bf16[640,4096]{1,0:T(8,128)(2,1)} fusion(bf16[1,4096,384]{2,1,0:T(8,128)(2,1)S(1)} %copy-done, bf16[640,4096]{1,0:T(8,128)(2,1)} %bitcast.44, bf16[1,4096,384]{2,1,0:T(8,128)(2,1)} %param.14, f32[640,384]{1,0:T(8,128)} %fusion.5), kind=kOutput, calls=%fused_computation.2 | convolution fusion | flops 4030627840 | bytes 17760256 | tf_op jit(solution)/shard_map/dot_general | solution.py:54
  165.3 120.1 %all_to_all.11 = bf16[16,40,4096]{2,1,0:T(8,128)(2,1)S(1)} all-to-all(bf16[16,40,4096]{2,1,0:T(8,128)(2,1)} %bitcast.45), channel_id=1, replica_groups=mesh['parts'=2,'expert'=16] {'expert'}, dimensions={0} | all-to-all | bytes 10485760 | tf_op jit(solution)/shard_map/all_to_all | solution.py:58
  285.4 6.4 %copy.9 = bf16[4,4,40,4096]{3,1,2,0:T(4,128)(2,1)} copy(bf16[4,4,40,4096]{3,2,1,0:T(8,128)(2,1)S(1)} %bitcast.42) | data formatting | bytes 10485760 | tf_op jit(solution)/shard_map/reshape | solution.py:59
  291.8 0.0 copy-start.2
  291.8 0.0 copy-start.3
  291.8 6.1 %gather_fusion = bf16[64,4,4096]{2,1,0:T(4,128)(2,1)} fusion(bf16[4,4,40,4096]{3,1,2,0:T(4,128)(2,1)} %copy.9, s32[64]{0:T(128)S(1)} %bitcast.46), kind=kCustom, calls=%fused_computation | custom fusion | bytes 4194816 | tf_op jit(solution)/shard_map/gather | solution.py:59
  297.9 4.4 %convert_reduce_fusion = f32[64,4096]{1,0:T(8,128)S(1)} fusion(bf16[64,4,4096]{2,1,0:T(4,128)(2,1)} %gather_fusion), kind=kLoop, calls=%fused_computation.6 | loop fusion | flops 1835008 | bytes 3145728 | tf_op jit(solution)/shard_map/reduce_sum | solution.py:60
  302.3 0.0 copy-done.2
  302.3 0.0 copy-done.3
  302.4 1.6 fusion.13
  (1 shorter events, 0.0 us)
Async XLA Ops:
  0.0 153.7 %copy-start = (bf16[1,4096,384]{2,1,0:T(8,128)(2,1)S(1)}, bf16[1,4096,384]{2,1,0:T(8,128)(2,1)}, u32[]{:S(2)}) copy-start(bf16[1,4096,384]{2,1,0:T(8,128)(2,1)} %param.15) | copy-start | bytes 9437188
  25.4 124.5 %copy-start.4 = (bf16[1,4096,384]{2,1,0:T(8,128)(2,1)S(1)}, bf16[1,4096,384]{2,1,0:T(8,128)(2,1)}, u32[]{:S(2)}) copy-start(bf16[1,4096,384]{2,1,0:T(8,128)(2,1)} %param.13) | copy-start | bytes 9437188
  147.6 2.3 copy-start.1
  291.8 10.5 %copy-start.2 = (f32[2,4096]{1,0:T(2,128)S(1)}, f32[2,4096]{1,0:T(2,128)}, u32[]{:S(2)}) copy-start(f32[2,4096]{1,0:T(2,128)} %param.12) | copy-start | bytes 98308
  291.8 10.6 %copy-start.3 = (f32[8,8]{1,0:T(8,128)S(1)}, f32[8,8]{1,0:T(8,128)}, u32[]{:S(2)}) copy-start(f32[8,8]{1,0:T(8,128)} %param.10) | copy-start | bytes 772
where the time goes:
time: 305 us; the launch traced here: 304 us
  blocking collectives  242 us (79%)
  local copies, waits for them, and re-layouts  39.2 us (13%)
  matrix products  17 us (6%)
  other arithmetic  5.45 us (2%)
    all_to_all x1, blocking collectives, local(): lax.all_to_all(outgoing_rows, 'expert', split_axis=0, concat_axis=0, tile...  122 us
    all_to_all x1, blocking collectives, local(): lax.all_to_all(partial_value, 'expert', split_axis=0, concat_axis=0, tile...  120 us
    scatter x1, local copies, waits for them, and re-layouts, local(): buffer = jnp.zeros((replicas, capacity, model_width), jnp.bfloat16).at[pa...  17.8 us
    dot_general x1, matrix products, local(): lax.dot_general(hidden, host_down, (((1,), (1,)), ((), ())), preferred_el...  11.6 us
    reshape x1, local copies, waits for them, and re-layouts, local(): returned.reshape(replicas, SPLIT, capacity, model_width)  6.39 us

commit v1 on v0

v1 whole, which is shorter than its diff:
```python
import functools

import jax
import jax.numpy as jnp
from jax import lax
from jax.experimental import pallas as pl
from jax.experimental.pallas import tpu as pltpu
from jax.sharding import PartitionSpec as P

SPLIT = 4
ROW_BLOCK = 16
IN_CHUNKS = 4
OUT_CHUNKS = 4
MESH = pl.DeviceIdType.MESH


def kernel(
    tokens_ref,
    assign_ref,
    router_ref,
    plan_ref,
    bias_ref,
    gate_hbm,
    up_hbm,
    down_hbm,
    out_ref,
    xbuf,
    w_in,
    w_down,
    acc,
    hidden,
    own_core,
    send_core,
    recv_core,
    own_y,
    send_y,
    recv_y,
    own_z,
    send_z,
    recv_z,
    own_sem,
    w_in_sem,
    w_down_sem,
    in_z_send,
    in_z_recv,
    in_y_send,
    in_y_recv,
    in_c_send,
    in_c_recv,
    out_c_send,
    out_c_recv,
    out_y_send,
    out_y_recv,
    out_z_send,
    out_z_recv,
):
    n = lax.axis_size("expert")
    reps = n // SPLIT
    me = lax.axis_index("expert")
    rep = me // SPLIT
    core_peer = me + 1 - 2 * (me % 2)
    y_peer = me + 2 - 4 * ((me // 2) % 2)

    def z_peer(k):
        return (me + k * SPLIT) % n

    slots = xbuf.shape[1]
    in_width = xbuf.shape[3]
    out_width = recv_z.shape[3]
    units = hidden.shape[1]
    tok = xbuf.shape[2]
    in_chunks, out_chunks = xbuf.shape[0], recv_z.shape[0]

    def remote(src, dst, send_sem, recv_sem, peer):
        return pltpu.make_async_remote_copy(
            src_ref=src,
            dst_ref=dst,
            send_sem=send_sem,
            recv_sem=recv_sem,
            device_id={"expert": peer},
            device_id_type=MESH,
        )

    def own_copy(c):
        return pltpu.make_async_copy(
            tokens_ref.at[:, pl.ds(c * in_width, in_width)], xbuf.at[c, 0], own_sem.at[c]
        )

    def w_copies(c):
        rows = pl.ds(c * in_width, in_width)
        return [
            pltpu.make_async_copy(
                gate_hbm.at[0, rows, :], w_in.at[rows, pl.ds(0, units)], w_in_sem.at[c, 0]
            ),
            pltpu.make_async_copy(
                up_hbm.at[0, rows, :], w_in.at[rows, pl.ds(units, units)], w_in_sem.at[c, 1]
            ),
        ]

    def down_copy(c):
        rows = pl.ds(c * out_width, out_width)
        return pltpu.make_async_copy(down_hbm.at[0, rows, :], w_down.at[rows, :], w_down_sem.at[c])

    for c in range(in_chunks):
        own_copy(c).start()
    for c in range(in_chunks):
        for copy in w_copies(c):
            copy.start()
    for c in range(out_chunks):
        down_copy(c).start()

    barrier = pltpu.get_barrier_semaphore()
    peers = [core_peer, y_peer] + [z_peer(k) for k in range(1, reps)]
    for peer in peers:
        pl.semaphore_signal(barrier, inc=1, device_id={"expert": peer}, device_id_type=MESH)
    pl.semaphore_wait(barrier, len(peers))

    def in_z(c, k):
        return remote(
            xbuf.at[c, 0],
            xbuf.at[c, reps - k],
            in_z_send.at[c, k],
            in_z_recv.at[c, reps - k],
            z_peer(k),
        )

    def in_y(c, k):
        return remote(
            xbuf.at[c, k], xbuf.at[c, reps + k], in_y_send.at[c, k], in_y_recv.at[c, k], y_peer
        )

    def in_c(c, k):
        return remote(
            xbuf.at[c, k],
            xbuf.at[c, 2 * reps + k],
            in_c_send.at[c, k],
            in_c_recv.at[c, k],
            core_peer,
        )

    order = sorted(range(1, reps), key=lambda k: min(k, reps - k))
    for c in range(in_chunks):
        own_copy(c).wait()
        for k in order:
            in_z(c, k).start()
        in_y(c, 0).start()
        in_c(c, 0).start()

    assign = assign_ref[...]
    router = router_ref[...]
    slot_expert = jnp.zeros_like(assign)
    for r in range(reps):
        slot_expert = jnp.where(assign == r, plan_ref[r], slot_expert)

    def replica_weight(k):
        return jnp.sum(
            jnp.where(assign == (rep + k) % reps, router, 0.0), axis=1, keepdims=True
        )

    def expert_weight(e):
        return jnp.sum(jnp.where(slot_expert == e, router, 0.0), axis=1, keepdims=True)

    def pass_on(c):
        for k in order:
            in_z(c, reps - k).wait_recv()
            in_y(c, k).start()
            in_c(c, k).start()
        for k in [0] + order:
            in_y(c, k).wait_recv()
            in_c(c, reps + k).start()

    row_blocks = slots // ROW_BLOCK
    rows_step = ROW_BLOCK * tok

    def multiply_in(c):
        for copy in w_copies(c):
            copy.wait()
        for k in [0] + order:
            in_c(c, k).wait_recv()
        for k in [0] + order:
            in_c(c, reps + k).wait_recv()

        def step(i, carry):
            x = xbuf[c, pl.ds(i * ROW_BLOCK, ROW_BLOCK)]
            x = x.astype(jnp.float32).reshape(rows_step, in_width).astype(jnp.bfloat16)
            w = w_in[pl.ds(c * in_width, in_width), :]
            product = jnp.dot(x, w, preferred_element_type=jnp.float32)
            if c == 0:
                acc[i] = product
            else:
                acc[i] = acc[i] + product
            return carry

        if row_blocks == 1:
            step(0, 0)
        else:
            lax.fori_loop(0, row_blocks, step, 0)

    for c in range(in_chunks):
        pass_on(c)
        if c > 0:
            multiply_in(c - 1)
    multiply_in(in_chunks - 1)

    def activate(i, carry):
        both = acc[i]
        gate = both[:, :units]
        up = both[:, units:]
        value = (gate / (1.0 + jnp.exp(-gate)) * up).astype(jnp.bfloat16)
        hidden[pl.ds(pl.multiple_of(i * rows_step, rows_step), rows_step), :] = value
        return carry

    if row_blocks == 1:
        activate(0, 0)
    else:
        lax.fori_loop(0, row_blocks, activate, 0)

    def out_c(c):
        return remote(
            send_core.at[c], recv_core.at[c], out_c_send.at[c], out_c_recv.at[c], core_peer
        )

    def out_y(c):
        return remote(send_y.at[c], recv_y.at[c], out_y_send.at[c], out_y_recv.at[c], y_peer)

    def out_z(c, k):
        return remote(
            send_z.at[c, k],
            recv_z.at[c, reps - k],
            out_z_send.at[c, k],
            out_z_recv.at[c, reps - k],
            z_peer(k),
        )

    half = slots // 2

    def multiply_out(c):
        down_copy(c).wait()
        w = w_down[pl.ds(c * out_width, out_width), :]

        def product(first_slot, count):
            h = hidden[pl.ds(pl.multiple_of(first_slot * tok, 16), count * tok), :]
            p = lax.dot_general(
                h, w, (((1,), (1,)), ((), ())), preferred_element_type=jnp.float32
            )
            return p.reshape(count, tok, out_width)

        if half < ROW_BLOCK:
            p = product(0, slots)
            send_core[c] = p[half:].astype(jnp.bfloat16)
            out_c(c).start()
            own_core[c] = p[:half]
        else:
            def step(i, carry):
                at = pl.ds(i * ROW_BLOCK, ROW_BLOCK)
                send_core[c, at] = product(half + i * ROW_BLOCK, ROW_BLOCK).astype(jnp.bfloat16)
                own_core[c, at] = product(i * ROW_BLOCK, ROW_BLOCK)
                return carry

            lax.fori_loop(0, half // ROW_BLOCK, step, 0)
            out_c(c).start()

    def sum_cores(c):
        out_c(c).wait_recv()
        send_y[c] = (
            own_core[c, pl.ds(reps, reps)]
            + recv_core[c, pl.ds(reps, reps)].astype(jnp.float32)
        ).astype(jnp.bfloat16)
        out_y(c).start()
        own_y[c] = own_core[c, pl.ds(0, reps)] + recv_core[c, pl.ds(0, reps)].astype(jnp.float32)

    def sum_y(c):
        out_y(c).wait_recv()
        for k in order:
            send_z[c, k] = (own_y[c, k] + recv_y[c, k].astype(jnp.float32)).astype(jnp.bfloat16)
            out_z(c, k).start()
        own_z[c] = own_y[c, 0] + recv_y[c, 0].astype(jnp.float32)

    def finish(c):
        columns = pl.ds(c * out_width, out_width)
        total = replica_weight(0) * own_z[c]
        for e in range(bias_ref.shape[0]):
            total = total + expert_weight(e) * bias_ref[pl.ds(e, 1), columns]
        for k in order:
            out_z(c, reps - k).wait_recv()
            total = total + replica_weight(k) * recv_z[c, k].astype(jnp.float32)
        out_ref[:, columns] = total.astype(jnp.bfloat16)

    for s in range(out_chunks + 3):
        if s < out_chunks:
            multiply_out(s)
        if 0 <= s - 1 < out_chunks:
            sum_cores(s - 1)
        if 0 <= s - 2 < out_chunks:
            sum_y(s - 2)
        if 0 <= s - 3 < out_chunks:
            finish(s - 3)

    for c in range(in_chunks):
        for k in range(1, reps):
            in_z(c, k).wait_send()
        for k in range(reps):
            in_y(c, k).wait_send()
        for k in range(2 * reps):
            in_c(c, k).wait_send()
    for c in range(out_chunks):
        out_c(c).wait_send()
        out_y(c).wait_send()
        for k in range(1, reps):
            out_z(c, k).wait_send()


def local(
    tokens,
    assignments,
    router_gates,
    replica_plan,
    expert_bias,
    gate_weight,
    up_weight,
    down_weight,
):
    n = lax.axis_size("expert")
    tok, width = tokens.shape
    units = gate_weight.shape[2]
    reps = n // SPLIT
    ci, co = IN_CHUNKS, OUT_CHUNKS
    wi, wo = width // ci, width // co
    half = n // 2
    row_blocks = n // ROW_BLOCK
    vmem = pl.BlockSpec(memory_space=pltpu.VMEM)
    smem = pl.BlockSpec(memory_space=pltpu.SMEM)
    hbm = pl.BlockSpec(memory_space=pltpu.HBM)
    dma = pltpu.SemaphoreType.DMA
    bf16, f32 = jnp.bfloat16, jnp.float32
    return pl.pallas_call(
        kernel,
        out_shape=jax.ShapeDtypeStruct((tok, width), bf16),
        in_specs=[hbm, vmem, vmem, smem, vmem, hbm, hbm, hbm],
        out_specs=vmem,
        scratch_shapes=[
            pltpu.VMEM((ci, n, tok, wi), bf16),
            pltpu.VMEM((width, 2 * units), bf16),
            pltpu.VMEM((width, units), bf16),
            pltpu.VMEM((row_blocks, ROW_BLOCK * tok, 2 * units), f32),
            pltpu.VMEM((n * tok, units), bf16),
            pltpu.VMEM((co, half, tok, wo), f32),
            pltpu.VMEM((co, half, tok, wo), bf16),
            pltpu.VMEM((co, half, tok, wo), bf16),
            pltpu.VMEM((co, reps, tok, wo), f32),
            pltpu.VMEM((co, reps, tok, wo), bf16),
            pltpu.VMEM((co, reps, tok, wo), bf16),
            pltpu.VMEM((co, tok, wo), f32),
            pltpu.VMEM((co, reps, tok, wo), bf16),
            pltpu.VMEM((co, reps, tok, wo), bf16),
            dma((ci,)),
            dma((ci, 2)),
            dma((co,)),
            dma((ci, reps)),
            dma((ci, reps)),
            dma((ci, reps)),
            dma((ci, reps)),
            dma((ci, 2 * reps)),
            dma((ci, 2 * reps)),
            dma((co,)),
            dma((co,)),
            dma((co,)),
            dma((co,)),
            dma((co, reps)),
            dma((co, reps)),
        ],
        compiler_params=pltpu.CompilerParams(
            collective_id=0, has_side_effects=True, vmem_limit_bytes=60 * 1024 * 1024
        ),
        cost_estimate=pl.CostEstimate(
            flops=6 * n * tok * width * units,
            bytes_accessed=6 * width * units,
            transcendentals=n * tok * units,
        ),
        name="routed_experts",
    )(
        tokens,
        assignments,
        router_gates,
        replica_plan,
        expert_bias,
        gate_weight,
        up_weight,
        down_weight,
    )


def solution(mesh):
    in_specs = (
        P(("parts", "expert"), None),
        P(("parts", "expert"), None),
        P(("parts", "expert"), None),
        P(),
        P(),
        P("expert", None, None),
        P("expert", None, None),
        P("expert", None, None),
    )
    out_specs = P(("parts", "expert"), None)
    return jax.shard_map(local, mesh=mesh, in_specs=in_specs, out_specs=out_specs, check_vma=False)
```

time: 305 us -> 44.3 us (0.15)
  blocking collectives: 242 us -> 0 us
  Pallas kernels: 0 us -> 42.6 us
  local copies, waits for them, and re-layouts: 39.2 us -> 1.47 us
  matrix products: 17 us -> 0 us
  other arithmetic: 5.45 us -> 0 us
    all_to_all x2 -> x0, blocking collectives: 242 us -> none  [the longest x1 122 us: local(): lax.all_to_all(outgoing_rows, 'expert', split_axis=0, concat_axis=0, tile...]
    pallas_call x0 -> x1, Pallas kernels: none -> 42.6 us  [local(): pl.pallas_call(kernel, out_shape=jax.ShapeDtypeStruct((tok, width), bf16)...]
    scatter x1 -> x0, local copies, waits for them, and re-layouts: 17.8 us -> none  [local(): buffer = jnp.zeros((replicas, capacity, model_width), jnp.bfloat16).at[pa...]
    dot_general x3 -> x0, matrix products: 17 us -> none  [the longest x1 11.6 us: local(): lax.dot_general(hidden, host_down, (((1,), (1,)), ((), ())), preferred_el...]
    reshape x3 -> x0, local copies, waits for them, and re-layouts: 8.93 us -> none  [the longest x1 6.39 us: local(): returned.reshape(replicas, SPLIT, capacity, model_width)]
    gather x1 -> x0, local copies, waits for them, and re-layouts: 6.09 us -> none  [local(): returned.reshape(replicas, SPLIT, capacity, model_width)]
    reduce_sum x2 -> x0, other arithmetic: 5.28 us -> none  [the longest x1 4.45 us: local(): combined = jnp.sum(gathered.astype(jnp.float32), axis=1)]
    broadcast_in_dim x2 -> x0, local copies, waits for them, and re-layouts: 3.15 us -> none  [the longest x1 1.95 us: local(): jnp.broadcast_to(buffer[:, None], (replicas, SPLIT, capacity, model_width))]
where the time goes in v1:
time: 44.3 us; the launch traced here: 44 us
  Pallas kernels  42.6 us (96%)
  local copies, waits for them, and re-layouts  1.47 us (3%)
    pallas_call x1, Pallas kernels, local(): pl.pallas_call(kernel, out_shape=jax.ShapeDtypeStruct((tok, width), bf16)...  42.6 us
    unnamed x1, local copies, waits for them, and re-layouts  1.47 us

profile of v1, /device:TPU:0, one launch (start us, length us, event | category | flops | bytes accessed | tf_op | source)
XLA Modules:
  0.0 44.0 jit_solution(11181750315848175411)
XLA Ops:
  0.0 42.6 %routed_experts.1 = bf16[8,4096]{1,0:T(8,128)(2,1)} custom-call(bf16[8,4096]{1,0:T(8,128)(2,1)} %tokens_ref.1, s32[8,8]{1,0:T(8,128)} %assign_ref.1, f32[8,8]{1,0:T(8,128)} %router_ref.1, s32[4]{0:T(128)} %plan_ref.1, f32[2,4096]{1,0:T(2,128)} %bias_ref.1, bf16[1,4096,384]{2,1,0:T(8,128)(2,1)} %gate_hbm.1, bf16[1,4096,384]{2,1,0:T(8,128)(2,1)} %up_hbm.1, ...), custom_call_target="tpu_custom_call" | custom-call | flops 1207959552 | bytes 9437184 | tf_op jit(solution)/shard_map/routed_experts/pallas_call | solution.py:336
  42.6 1.5 %copy.10 = bf16[8,4096]{1,0:T(8,128)(2,1)} copy(bf16[8,4096]{1,0:T(8,128)(2,1)} %routed_experts.1) | data formatting | bytes 131072

commit v2 on v1

--- a/solution.py
+++ b/solution.py
@@ -9,20 +9,25 @@
 
 SPLIT = 4
 ROW_BLOCK = 16
-IN_CHUNKS = 4
+IN_CHUNKS = 2
 OUT_CHUNKS = 4
 MESH = pl.DeviceIdType.MESH
 
 
 def kernel(
     tokens_ref,
+    assign_hbm,
+    router_hbm,
+    plan_hbm,
+    bias_hbm,
+    gate_hbm,
+    up_hbm,
+    down_hbm,
+    out_hbm,
     assign_ref,
     router_ref,
     plan_ref,
     bias_ref,
-    gate_hbm,
-    up_hbm,
-    down_hbm,
     out_ref,
     xbuf,
     w_in,
@@ -38,6 +43,8 @@
     own_z,
     send_z,
     recv_z,
+    small_sem,
+    out_sem,
     own_sem,
     w_in_sem,
     w_down_sem,
@@ -108,6 +115,19 @@
             copy.start()
     for c in range(out_chunks):
         down_copy(c).start()
+    small_copies = [
+        pltpu.make_async_copy(src, dst, small_sem.at[i])
+        for i, (src, dst) in enumerate(
+            [
+                (assign_hbm, assign_ref),
+                (router_hbm, router_ref),
+                (plan_hbm, plan_ref),
+                (bias_hbm, bias_ref),
+            ]
+        )
+    ]
+    for copy in small_copies:
+        copy.start()
 
     barrier = pltpu.get_barrier_semaphore()
     peers = [core_peer, y_peer] + [z_peer(k) for k in range(1, reps)]
@@ -146,6 +166,9 @@
         in_y(c, 0).start()
         in_c(c, 0).start()
 
+    for copy in small_copies:
+        copy.wait()
+
     assign = assign_ref[...]
     router = router_ref[...]
     slot_expert = jnp.zeros_like(assign)
@@ -160,11 +183,13 @@
     def expert_weight(e):
         return jnp.sum(jnp.where(slot_expert == e, router, 0.0), axis=1, keepdims=True)
 
-    def pass_on(c):
+    def pass_z(c):
         for k in order:
             in_z(c, reps - k).wait_recv()
             in_y(c, k).start()
             in_c(c, k).start()
+
+    def pass_y(c):
         for k in [0] + order:
             in_y(c, k).wait_recv()
             in_c(c, reps + k).start()
@@ -197,7 +222,9 @@
             lax.fori_loop(0, row_blocks, step, 0)
 
     for c in range(in_chunks):
-        pass_on(c)
+        pass_z(c)
+    for c in range(in_chunks):
+        pass_y(c)
         if c > 0:
             multiply_in(c - 1)
     multiply_in(in_chunks - 1)
@@ -231,6 +258,10 @@
             out_z_recv.at[c, reps - k],
             z_peer(k),
         )
+
+    def out_copy(c):
+        columns = pl.ds(c * out_width, out_width)
+        return pltpu.make_async_copy(out_ref.at[:, columns], out_hbm.at[:, columns], out_sem.at[c])
 
     half = slots // 2
 
@@ -285,16 +316,17 @@
             out_z(c, reps - k).wait_recv()
             total = total + replica_weight(k) * recv_z[c, k].astype(jnp.float32)
         out_ref[:, columns] = total.astype(jnp.bfloat16)
-
-    for s in range(out_chunks + 3):
-        if s < out_chunks:
-            multiply_out(s)
-        if 0 <= s - 1 < out_chunks:
-            sum_cores(s - 1)
-        if 0 <= s - 2 < out_chunks:
-            sum_y(s - 2)
-        if 0 <= s - 3 < out_chunks:
-            finish(s - 3)
+        out_copy(c).start()
+
+    for c in range(out_chunks):
+        multiply_out(c)
+        if c > 0:
+            sum_cores(c - 1)
+    sum_cores(out_chunks - 1)
+    for c in range(out_chunks):
+        sum_y(c)
+    for c in range(out_chunks):
+        finish(c)
 
     for c in range(in_chunks):
         for k in range(1, reps):
@@ -308,6 +340,7 @@
         out_y(c).wait_send()
         for k in range(1, reps):
             out_z(c, k).wait_send()
+        out_copy(c).wait()
 
 
 def local(
@@ -328,17 +361,20 @@
     wi, wo = width // ci, width // co
     half = n // 2
     row_blocks = n // ROW_BLOCK
-    vmem = pl.BlockSpec(memory_space=pltpu.VMEM)
-    smem = pl.BlockSpec(memory_space=pltpu.SMEM)
     hbm = pl.BlockSpec(memory_space=pltpu.HBM)
     dma = pltpu.SemaphoreType.DMA
     bf16, f32 = jnp.bfloat16, jnp.float32
     return pl.pallas_call(
         kernel,
         out_shape=jax.ShapeDtypeStruct((tok, width), bf16),
-        in_specs=[hbm, vmem, vmem, smem, vmem, hbm, hbm, hbm],
-        out_specs=vmem,
+        in_specs=[hbm] * 8,
+        out_specs=hbm,
         scratch_shapes=[
+            pltpu.VMEM(assignments.shape, jnp.int32),
+            pltpu.VMEM(router_gates.shape, f32),
+            pltpu.SMEM(replica_plan.shape, jnp.int32),
+            pltpu.VMEM(expert_bias.shape, f32),
+            pltpu.VMEM((tok, width), bf16),
             pltpu.VMEM((ci, n, tok, wi), bf16),
             pltpu.VMEM((width, 2 * units), bf16),
             pltpu.VMEM((width, units), bf16),
@@ -353,6 +389,8 @@
             pltpu.VMEM((co, tok, wo), f32),
             pltpu.VMEM((co, reps, tok, wo), bf16),
             pltpu.VMEM((co, reps, tok, wo), bf16),
+            dma((4,)),
+            dma((co,)),
             dma((ci,)),
             dma((ci, 2)),
             dma((co,)),

time: 44.3 us -> 32.9 us (0.74)
  Pallas kernels: 42.6 us -> 31.3 us
    pallas_call x1, Pallas kernels: 42.6 us -> 31.3 us  [local(): pl.pallas_call(kernel, out_shape=jax.ShapeDtypeStruct((tok, width), bf16)...]
where the time goes in v2:
time: 32.9 us; the launch traced here: 32.8 us
  Pallas kernels  31.3 us (95%)
  local copies, waits for them, and re-layouts  1.47 us (4%)
    pallas_call x1, Pallas kernels, local(): pl.pallas_call(kernel, out_shape=jax.ShapeDtypeStruct((tok, width), bf16)...  31.3 us
    unnamed x1, local copies, waits for them, and re-layouts  1.47 us

profile of v2, /device:TPU:0, one launch (start us, length us, event | category | flops | bytes accessed | tf_op | source)
XLA Modules:
  0.0 32.8 jit_solution(16351626636100337211)
XLA Ops:
  0.0 31.3 %routed_experts.1 = bf16[8,4096]{1,0:T(8,128)(2,1)} custom-call(bf16[8,4096]{1,0:T(8,128)(2,1)} %tokens_ref.1, s32[8,8]{1,0:T(8,128)} %assign_hbm.1, f32[8,8]{1,0:T(8,128)} %router_hbm.1, s32[4]{0:T(128)} %plan_hbm.1, f32[2,4096]{1,0:T(2,128)} %bias_hbm.1, bf16[1,4096,384]{2,1,0:T(8,128)(2,1)} %gate_hbm.1, bf16[1,4096,384]{2,1,0:T(8,128)(2,1)} %up_hbm.1, ...), custom_call_target="tpu_custom_call" | custom-call | flops 1207959552 | bytes 9437184 | tf_op jit(solution)/shard_map/routed_experts/pallas_call | solution.py:367
  31.3 1.5 %copy.10 = bf16[8,4096]{1,0:T(8,128)(2,1)} copy(bf16[8,4096]{1,0:T(8,128)(2,1)} %routed_experts.1) | data formatting | bytes 131072

commit v3 on v2

--- a/solution.py
+++ b/solution.py
@@ -149,12 +149,12 @@
             xbuf.at[c, k], xbuf.at[c, reps + k], in_y_send.at[c, k], in_y_recv.at[c, k], y_peer
         )
 
-    def in_c(c, k):
+    def in_c(c, y):
         return remote(
-            xbuf.at[c, k],
-            xbuf.at[c, 2 * reps + k],
-            in_c_send.at[c, k],
-            in_c_recv.at[c, k],
+            xbuf.at[c, pl.ds(y * reps, reps)],
+            xbuf.at[c, pl.ds((2 + y) * reps, reps)],
+            in_c_send.at[c, y],
+            in_c_recv.at[c, y],
             core_peer,
         )
 
@@ -164,7 +164,6 @@
         for k in order:
             in_z(c, k).start()
         in_y(c, 0).start()
-        in_c(c, 0).start()
 
     for copy in small_copies:
         copy.wait()
@@ -187,12 +186,12 @@
         for k in order:
             in_z(c, reps - k).wait_recv()
             in_y(c, k).start()
-            in_c(c, k).start()
+        in_c(c, 0).start()
 
     def pass_y(c):
         for k in [0] + order:
             in_y(c, k).wait_recv()
-            in_c(c, reps + k).start()
+        in_c(c, 1).start()
 
     row_blocks = slots // ROW_BLOCK
     rows_step = ROW_BLOCK * tok
@@ -200,10 +199,8 @@
     def multiply_in(c):
         for copy in w_copies(c):
             copy.wait()
-        for k in [0] + order:
-            in_c(c, k).wait_recv()
-        for k in [0] + order:
-            in_c(c, reps + k).wait_recv()
+        in_c(c, 0).wait_recv()
+        in_c(c, 1).wait_recv()
 
         def step(i, carry):
             x = xbuf[c, pl.ds(i * ROW_BLOCK, ROW_BLOCK)]
@@ -333,8 +330,8 @@
             in_z(c, k).wait_send()
         for k in range(reps):
             in_y(c, k).wait_send()
-        for k in range(2 * reps):
-            in_c(c, k).wait_send()
+        in_c(c, 0).wait_send()
+        in_c(c, 1).wait_send()
     for c in range(out_chunks):
         out_c(c).wait_send()
         out_y(c).wait_send()
@@ -398,8 +395,8 @@
             dma((ci, reps)),
             dma((ci, reps)),
             dma((ci, reps)),
-            dma((ci, 2 * reps)),
-            dma((ci, 2 * reps)),
+            dma((ci, 2)),
+            dma((ci, 2)),
             dma((co,)),
             dma((co,)),
             dma((co,)),

time: 32.9 us -> 32.7 us (level)
  no operation moved by 1% of the time
where the time goes in v3:
time: 32.7 us; the launch traced here: 32.5 us
  Pallas kernels  31 us (95%)
  local copies, waits for them, and re-layouts  1.47 us (4%)
    pallas_call x1, Pallas kernels, local(): pl.pallas_call(kernel, out_shape=jax.ShapeDtypeStruct((tok, width), bf16)...  31 us
    unnamed x1, local copies, waits for them, and re-layouts  1.47 us

profile of v3, /device:TPU:0, one launch (start us, length us, event | category | flops | bytes accessed | tf_op | source)
XLA Modules:
  0.0 32.5 jit_solution(16064464983019774702)
XLA Ops:
  0.0 31.0 %routed_experts.1 = bf16[8,4096]{1,0:T(8,128)(2,1)} custom-call(bf16[8,4096]{1,0:T(8,128)(2,1)} %tokens_ref.1, s32[8,8]{1,0:T(8,128)} %assign_hbm.1, f32[8,8]{1,0:T(8,128)} %router_hbm.1, s32[4]{0:T(128)} %plan_hbm.1, f32[2,4096]{1,0:T(2,128)} %bias_hbm.1, bf16[1,4096,384]{2,1,0:T(8,128)(2,1)} %gate_hbm.1, bf16[1,4096,384]{2,1,0:T(8,128)(2,1)} %up_hbm.1, ...), custom_call_target="tpu_custom_call" | custom-call | flops 1207959552 | bytes 9437184 | tf_op jit(solution)/shard_map/routed_experts/pallas_call | solution.py:364
  31.0 1.5 %copy.10 = bf16[8,4096]{1,0:T(8,128)(2,1)} copy(bf16[8,4096]{1,0:T(8,128)(2,1)} %routed_experts.1) | data formatting | bytes 131072
